TPU v7x, 32 devices: a whole 2x2x4 slice. The times are simulated.
32 devices in a mesh: ctx: 8 (over z, y), tp: 4 (over x, core).
Axes of the slice: x: 2, y: 2, z: 4, core: 2. Of those that a mesh axis runs over, the one named last changes fastest.
Arguments:
- queries: bfloat16 [12288, 8192], P('ctx', 'tp'), may hold values from -6 to 6
- keys: bfloat16 [12288, 8192], P('ctx', 'tp'), may hold values from -6 to 6
- values: bfloat16 [12288, 8192], P('ctx', 'tp'), may hold values from -180 to 180
- gain: float32 [8192], P('tp'), may hold values from 0.5 to 1.5
- starts: int32 [12288], P('ctx'), may hold values 0 or 1
- source_unit: int32 [128], replicated, may hold values from 0 to 127, as said below
Outputs:
- normed: bfloat16 [12288, 8192], P('ctx', 'tp')
Inputs may be any that keep to these rules, and one draw needn't show every extreme that they name: `source_unit`: A permutation of the units. The units of ctx index b are balanced units 2 * 8 * b to 2 * 8 * b + 2 * 8 - 1, and exactly 2 of them come from the units of each arrival index a (arrival units 2 * 8 * a to 2 * 8 * a + 2 * 8 - 1).
All inputs are finite; a program needn't handle non-finite values. No bound on the sum of `starts` on one device may be relied on, other than what follows from the above.
Results may differ from a plain program's by a relative error of at most 0.0053.
Values may be sent and summed in bfloat16 or wider, within the bound.
A program may use at most 128 MiB of HBM per device.

v0:
```python
import jax
import jax.numpy as jnp
from jax import lax
from jax.sharding import PartitionSpec as P

DH = 128
CAP = 2
BLK = 768


def local(queries, keys, values, gain, starts, source_unit):
    shard_count = lax.axis_size("ctx")
    my_index = lax.axis_index("ctx")
    token_count, column_count = queries.shape
    slot_count = 2 * shard_count
    unit_rows = token_count // slot_count
    head_count = column_count // DH
    owners = source_unit.reshape(shard_count, slot_count)
    source_shard = owners // slot_count
    source_slot = owners % slot_count
    earlier_slot = jnp.arange(slot_count)[None, :] < jnp.arange(slot_count)[:, None]
    same_source = source_shard[:, :, None] == source_shard[:, None, :]
    arrival_rank = jnp.sum(jnp.where(same_source & earlier_slot[None], 1, 0), axis=2).astype(
        jnp.int32
    )
    from_me = source_shard == my_index
    matches = from_me[:, None, :] & (
        arrival_rank[:, None, :] == jnp.arange(CAP, dtype=jnp.int32)[None, :, None]
    )
    chosen = jnp.sum(jnp.where(matches, source_slot[:, None, :], 0), axis=2).reshape(-1)
    occupied = jnp.any(matches, axis=2).reshape(-1)

    def packed(array):
        pieces = array.reshape(slot_count, unit_rows, column_count)[chosen]
        pieces = jnp.where(occupied[:, None, None], pieces, jnp.zeros_like(pieces))
        return pieces.reshape(shard_count, CAP * unit_rows, column_count)

    arrived = (
        lax.all_to_all(packed(queries), "ctx", split_axis=0, concat_axis=0, tiled=True),
        lax.all_to_all(packed(keys), "ctx", split_axis=0, concat_axis=0, tiled=True),
        lax.all_to_all(packed(values), "ctx", split_axis=0, concat_axis=0, tiled=True),
    )
    my_source = lax.dynamic_index_in_dim(source_shard, my_index, 0, keepdims=False)
    my_rank = lax.dynamic_index_in_dim(arrival_rank, my_index, 0, keepdims=False)
    lookup = my_source * CAP + my_rank

    def unpacked(array):
        return array.reshape(shard_count * CAP, unit_rows, column_count)[lookup].reshape(
            token_count, column_count
        )

    block_count = token_count // BLK
    q_feat = (
        jax.nn.silu(unpacked(arrived[0]).astype(jnp.float32))
        .astype(jnp.bfloat16)
        .reshape(block_count, BLK, head_count, DH)
    )
    k_feat = (
        jax.nn.silu(unpacked(arrived[1]).astype(jnp.float32))
        .astype(jnp.bfloat16)
        .reshape(block_count, BLK, head_count, DH)
    )
    v_bal = unpacked(arrived[2]).reshape(block_count, BLK, head_count, DH)
    block_starts = starts.reshape(block_count, BLK)
    local_doc = jnp.cumsum(starts).reshape(block_count, BLK)
    last_doc = local_doc[:, BLK - 1 :]
    recent = jnp.where((local_doc == last_doc)[:, :, None, None], k_feat, jnp.zeros_like(k_feat))
    block_states = jnp.einsum("bshd,bshe->bhde", recent, v_bal, preferred_element_type=jnp.float32)
    has_start = jnp.any(block_starts > 0, axis=1)
    opening = block_starts[:, 0] > 0
    running = jnp.zeros((head_count, DH, DH), jnp.float32)
    for position in range(block_count):
        running = jnp.where(has_start[position], 0.0, running) + block_states[position]
    shard_flag = jnp.any(starts > 0).astype(jnp.float32).reshape(1)
    all_flags = lax.all_gather(shard_flag, "ctx", axis=0, tiled=True)
    shard_ids = jnp.arange(shard_count, dtype=jnp.int32)
    lowest = jnp.max(jnp.where((shard_ids < my_index) & (all_flags > 0), shard_ids, 0))
    piece = lax.all_gather(running[None], "ctx", axis=0, tiled=True)
    ids = jnp.arange(piece.shape[0], dtype=jnp.int32)
    wanted = (ids >= lowest) & (ids < my_index)
    incoming = jnp.sum(jnp.where(wanted[:, None, None, None], piece, 0.0), axis=0)
    causal = jnp.tril(jnp.ones((BLK, BLK), dtype=bool))
    scores = jnp.einsum("bthd,bshd->bhts", q_feat, k_feat, preferred_element_type=jnp.float32)
    allowed = causal[None] & (local_doc[:, :, None] == local_doc[:, None, :])
    weights = jnp.where(allowed[:, None], scores, 0.0).astype(jnp.bfloat16)
    within = jnp.einsum("bhts,bshe->bthe", weights, v_bal, preferred_element_type=jnp.float32)
    carry_state = incoming
    carried_parts = []
    for position in range(block_count):
        entering = jnp.where(opening[position], 0.0, carry_state).astype(jnp.bfloat16)
        carried = jnp.einsum(
            "thd,hde->the", q_feat[position], entering, preferred_element_type=jnp.float32
        )
        seen = local_doc[position] == local_doc[position, 0]
        carried_parts.append(jnp.where(seen[:, None, None], carried, 0.0))
        carry_state = jnp.where(has_start[position], 0.0, carry_state) + block_states[position]
    attended = jnp.stack(carried_parts) + within
    flat = attended.reshape(token_count, column_count)
    square_sums = lax.psum(jnp.sum(flat * flat, axis=1), "tp")
    mean_square = square_sums / (column_count * lax.axis_size("tp"))
    return (flat * lax.rsqrt(mean_square + 1e-06)[:, None] * gain).astype(jnp.bfloat16)


def solution(mesh):
    in_specs = (P("ctx", "tp"), P("ctx", "tp"), P("ctx", "tp"), P("tp"), P("ctx"), P())
    out_specs = P("ctx", "tp")
    return jax.shard_map(local, mesh=mesh, in_specs=in_specs, out_specs=out_specs, check_vma=False)
```

profile of v0, /device:TPU:13, one launch (start us, length us, event | category | flops | bytes accessed | tf_op | source)
XLA Modules:
  0.0 661.7 jit_solution(13066329679675970164)
XLA Ops:
  6.5 0.7 reshape.362
  7.3 0.3 select_reduce_fusion.1
  7.6 0.2 fusion.38
  7.7 0.2 select_reduce_fusion.2
  8.1 6.4 gather_fusion
  14.5 6.4 gather_fusion.4
  20.9 6.4 gather_fusion.2
  27.6 12.2 %bitcast_select_fusion.2 = (bf16[8,192,2048]{2,1,0:T(8,128)(2,1)S(1)}, bf16[8,192,2048]{2,1,0:T(8,128)(2,1)}, bf16[8,192,2048]{2,1,0:T(8,128)(2,1)}) fusion(pred[8,192]{1,0:T(8,128)(4,1)S(1)} %broadcast_in_dim.142, bf16[8,192,2048]{2,1,0:T(8,128)(2,1)} %bitcast.125, bf16[8,192,2048]{2,1,0:T(8,128)(2,1)} %bitcast.127, bf16[8,192,2048]{2,1,0:T(8,128)(2,1)} %bitcast.126), kind=kLoop, calls=%fused_computation.37 | loop fusion | flops 9437184 | bytes 37750272 | tf_op jit(solution)/shard_map/jit(_where)/select_n | solution.py:35
  39.7 140.5 %all_to_all.15 = bf16[8,192,2048]{2,1,0:T(8,128)(2,1)} all-to-all(bf16[8,192,2048]{2,1,0:T(8,128)(2,1)S(1)} %get-tuple-element.15), channel_id=1, replica_groups=mesh['ctx'=8,'tp'=4] {'ctx'}, dimensions={0} | all-to-all | bytes 12582912 | tf_op jit(solution)/shard_map/all_to_all | solution.py:40
  180.3 7.1 %all-to-all-start.1 = ((bf16[8,192,2048]{2,1,0:T(8,128)(2,1)}), bf16[8,192,2048]{2,1,0:T(8,128)(2,1)}, u32[]{:S(2)}, u32[]{:S(2)}) async-start(bf16[8,192,2048]{2,1,0:T(8,128)(2,1)} %get-tuple-element.16), calls=%async_computation.1 | async-start | bytes 12582912 | tf_op jit(solution)/shard_map/all_to_all | solution.py:41
  187.4 0.3 reduce-window.9
  188.1 0.2 slice_reduce_fusion.1
  188.4 0.6 fusion.53
  189.1 6.4 gather_fusion.1
  195.5 9.7 %copy.115 = f32[192,8,16,128]{3,2,1,0:T(8,128)} copy(bf16[192,8,16,128]{3,1,2,0:T(8,128)(2,1)} %bitcast.130) | data formatting | bytes 18874368
  205.2 117.8 %all-to-all-done.1 = bf16[8,192,2048]{2,1,0:T(8,128)(2,1)} async-done(((bf16[8,192,2048]{2,1,0:T(8,128)(2,1)}), bf16[8,192,2048]{2,1,0:T(8,128)(2,1)}, u32[]{:S(2)}, u32[]{:S(2)}) %all-to-all-start.1) | async-done | bytes 6291488 | tf_op jit(solution)/shard_map/all_to_all | solution.py:41
  323.0 6.5 all-to-all-start.2
  329.4 6.4 gather_fusion.3
  335.9 7.8 %copy.116 = bf16[192,8,16,128]{3,2,1,0:T(8,128)(2,1)} copy(bf16[192,8,16,128]{3,1,2,0:T(8,128)(2,1)} %bitcast.128) | data formatting | bytes 12582912
  343.6 9.0 %copy.108 = bf16[2,768,16,128]{1,3,2,0:T(8,128)(2,1)} copy(bf16[2,768,16,128]{3,2,1,0:T(8,128)(2,1)} %bitcast.129) | data formatting | bytes 12582912 | tf_op jit(solution)/shard_map/reshape;reshape | solution.py:63
  352.6 11.4 %broadcast_select_fusion = (bf16[2,768,16,128]{3,2,1,0:T(8,128)(2,1)}, bf16[2,768,16,128]{3,2,1,0:T(8,128)(2,1)}) fusion(pred[2,768]{1,0:T(4,128)(4,1)S(1)} %broadcast_compare_fusion, f32[2,768,16,128]{3,2,1,0:T(8,128)} %bitcast.121), kind=kLoop, calls=%fused_computation.44 | loop fusion | flops 18874368 | bytes 25167360 | tf_op jit(solution)/shard_map/jit(_where)/select_n | solution.py:67
  364.0 6.9 %fusion.23 = f32[2,16,128,128]{3,2,1,0:T(8,128)S(1)} fusion(bf16[2,768,16,128]{1,3,2,0:T(8,128)(2,1)S(1)} %copy-done, bf16[2,768,16,128]{3,2,1,0:T(8,128)(2,1)} %get-tuple-element.5), kind=kOutput, calls=%fused_computation.40 | convolution fusion | flops 805306368 | bytes 14680064 | tf_op jit(solution)/shard_map/bshd,bshe->bhde/dot_general | solution.py:68
  371.0 1.6 slice_add_fusion
  372.6 0.6 compare_reduce_fusion.1
  373.9 0.6 dynamic-slice
  374.5 0.7 dynamic-update-slice
  375.3 161.1 %all-reduce = f32[8]{0:T(128)S(1)} all-reduce(f32[8]{0:T(128)S(1)} %dynamic-update-slice), channel_id=1, replica_groups=mesh['ctx'=8,'tp'=4] {'ctx'}, use_global_device_ids=true, to_apply=%add | all-reduce | flops 8 | bytes 64
  536.4 0.6 fusion.45
  537.0 0.6 compare_and_fusion.1
  537.6 0.5 fusion.51
  538.1 0.6 fusion.52
  538.7 0.2 iota_compare_fusion
  539.0 1.2 fusion.40
  540.2 1.0 compare_and_fusion
  541.2 6.3 gather_fusion.5
  547.6 6.4 fusion.16
  554.0 3.3 fusion.50
  557.3 4.7 copy.100
  562.0 4.7 copy.103
  566.7 5.0 copy.117
  571.7 4.9 fusion.18
  576.6 4.7 select_reduce_fusion
  581.3 4.6 select_bitcast_fusion.1
  585.9 4.9 select_bitcast_fusion
  590.8 30.5 %multiply_reduce_fusion = (f32[2,768]{1,0:T(2,128)S(1)}, f32[2,768,16,128]{1,3,2,0:T(8,128)}) fusion(bf16[2,768,16,128]{1,3,2,0:T(8,128)(2,1)} %copy.108, pred[2,768,768]{2,1,0:T(8,128)(4,1)S(1)} %compare_and_fusion, bf16[2,768,16,128]{3,2,1,0:T(8,128)(2,1)} %get-tuple-element.6, bf16[2,768,16,128]{3,2,1,0:T(8,128)(2,1)} %fusion.18, ...), kind=kOutput, calls=%fused_computation.30 | convolution fusion | flops 9714006016 | bytes 45225984 | tf_op jit(solution)/shard_map/bhts,bshe->bthe/dot_general | solution.py:86
  621.3 12.7 %copy.109 = f32[2,768,16,128]{3,2,1,0:T(8,128)} copy(f32[2,768,16,128]{1,3,2,0:T(8,128)} %get-tuple-element.23) | data formatting | bytes 25165824 | tf_op jit(solution)/shard_map/add | solution.py:97
  634.0 9.3 %psum.7 = f32[1536]{0:T(1024)S(1)} all-reduce(f32[1536]{0:T(1024)S(1)} %reduce_sum.42), channel_id=1, replica_groups=mesh['ctx'=8,'tp'=4] {'tp'}, use_global_device_ids=true, to_apply=%region_10.11 | all-reduce | flops 1536 | bytes 12288 | tf_op jit(solution)/shard_map/psum | solution.py:99
  643.4 11.5 %fusion.6 = bf16[1536,2048]{1,0:T(8,128)(2,1)} fusion(f32[192,8,16,128]{3,2,1,0:T(8,128)} %bitcast.123, f32[2048]{0:T(1024)S(1)} %copy-done.4, f32[1536]{0:T(1024)S(1)} %add_rsqrt_fusion), kind=kLoop, calls=%fused_computation.13 | loop fusion | flops 9437184 | bytes 18888704 | tf_op jit(solution)/shard_map/convert_element_type | solution.py:101
  (43 shorter events, 1.2 us)
Async XLA Ops:
  180.3 7.1 %copy-start.3 = (s32[1536]{0:T(1024)S(1)}, s32[1536]{0:T(1024)}, u32[]{:S(2)}) copy-start(s32[1536]{0:T(1024)} %param.10) | copy-start | bytes 18436
  180.3 142.7 %all-to-all-start.1 = ((bf16[8,192,2048]{2,1,0:T(8,128)(2,1)}), bf16[8,192,2048]{2,1,0:T(8,128)(2,1)}, u32[]{:S(2)}, u32[]{:S(2)}) async-start(bf16[8,192,2048]{2,1,0:T(8,128)(2,1)} %get-tuple-element.16), calls=%async_computation.1 | async-start | bytes 12582912 | tf_op jit(solution)/shard_map/all_to_all | solution.py:41
  323.0 218.3 %all-to-all-start.2 = ((bf16[8,192,2048]{2,1,0:T(8,128)(2,1)}), bf16[8,192,2048]{2,1,0:T(8,128)(2,1)}, u32[]{:S(2)}, u32[]{:S(2)}) async-start(bf16[8,192,2048]{2,1,0:T(8,128)(2,1)} %get-tuple-element.17), calls=%async_computation.2 | async-start | bytes 12582912 | tf_op jit(solution)/shard_map/all_to_all | solution.py:39
  329.4 247.2 %all-gather.2.cloned.1.call-start = ((), (), s32[]{:S(2)}) async-start(), calls=%async_computation.3 | async-start | bytes 9437184 | tf_op jit(solution)/shard_map/all_gather | solution.py:78
  352.6 11.5 %copy-start = (bf16[2,768,16,128]{1,3,2,0:T(8,128)(2,1)S(1)}, bf16[2,768,16,128]{1,3,2,0:T(8,128)(2,1)}, u32[]{:S(2)}) copy-start(bf16[2,768,16,128]{1,3,2,0:T(8,128)(2,1)} %copy.108) | copy-start | bytes 18874372
  364.0 9.9 %copy-start.5 = (u32[32]{0:T(128)S(1)}, u32[32]{0:T(128)}, u32[]{:S(2)}) copy-start(u32[32]{0:T(128)} %constant.78) | copy-start | bytes 388
  576.6 4.7 copy-start.2
  581.3 4.6 copy-start.1
  621.3 22.1 %copy-start.4 = (f32[2048]{0:T(1024)S(1)}, f32[2048]{0:T(1024)}, u32[]{:S(2)}) copy-start(f32[2048]{0:T(1024)} %param.9) | copy-start | bytes 24580
Sparse Core Ops, SparseCore 0:
  372.7 194.2 all-gather.1
where the time goes:
time: 668 us; the launch traced here: 662 us
  blocking collectives  311 us (47%)
  waiting for transfers between devices  118 us (18%)
  local copies, waits for them, and re-layouts  100 us (15%)
  other arithmetic  58.3 us (9%)
  matrix products  46.9 us (7%)
  between operations  14.2 us (2%)
  starting transfers between devices  13.6 us (2%)
    unnamed x1, blocking collectives  161 us
    all_to_all x1, blocking collectives, local(): lax.all_to_all(packed(keys), 'ctx', split_axis=0, concat_axis=0, tiled=True)  141 us
    all_to_all x1, waiting for transfers between devices, local(): lax.all_to_all(packed(values), 'ctx', split_axis=0, concat_axis=0, tiled=...  118 us
    dot_general x1, matrix products, local(): jnp.einsum('bhts,bshe->bthe', weights, v_bal, preferred_element_type=jnp....  30.5 us
    unnamed x19, local copies, waits for them, and re-layouts  23.9 us
    gather x3, local copies, waits for them, and re-layouts, packed(): pieces = array.reshape(slot_count, unit_rows, column_count)[chosen]  19.2 us
    gather x3, local copies, waits for them, and re-layouts, unpacked(): array.reshape(shard_count * CAP, unit_rows, column_count)[lookup]  19.2 us
  transfers between devices with their start and end apart: 3, of which 1 were waited for; matrix products, arithmetic and copies ran while one was open for 16% of the time, Pallas kernels for 0%

commit v1 on v0

--- a/solution.py
+++ b/solution.py
@@ -1,11 +1,336 @@
+import functools
 import jax
 import jax.numpy as jnp
 from jax import lax
+from jax.experimental import pallas as pl
+from jax.experimental.pallas import tpu as pltpu
 from jax.sharding import PartitionSpec as P
 
 DH = 128
 CAP = 2
 BLK = 768
+TILE = 256
+GROUPS = 4
+WINDOW = 2
+MESH = pl.DeviceIdType.MESH
+
+
+def silu(x):
+    x = x.astype(jnp.float32)
+    return (x / (1.0 + jnp.exp(-x))).astype(jnp.bfloat16)
+
+
+def exchange_kernel(
+    n, tp, q_in, k_in, v_in, chosen, lookup, flags, doc_col, doc_row,
+    out, sums, staged, packed, arrived, q_ord, k_ord, v_ord, chain_in, chain_out, block_state,
+    out_buf, squares, own_sum, tp_in,
+    stage_sem, send_sem, recv_sem, chain_send, chain_recv, out_sem, tp_send, tp_recv,
+):
+    me = lax.axis_index("ctx")
+    my_tp = lax.axis_index("tp")
+    slots, unit_rows, _ = q_in.shape
+    group_heads = q_ord.shape[0]
+    width = group_heads * DH
+    tokens = slots * unit_rows
+    blocks = tokens // BLK
+    sources = []
+    for g in range(GROUPS):
+        sources += [(k_in, g, True), (v_in, g, False)]
+    sources += [(q_in, g, True) for g in range(GROUPS)]
+    pieces = len(sources)
+
+    def stage(i):
+        ref, g, _ = sources[i]
+        return pltpu.make_async_copy(
+            ref.at[:, :, pl.ds(g * width, width)], staged[i % 2], stage_sem.at[i % 2]
+        )
+
+    def prepare(i):
+        stage(i).wait()
+        feature = sources[i][2]
+
+        def one(u, _):
+            rows = staged[i % 2][chosen[u]]
+            rows = silu(rows) if feature else rows
+            for h in range(group_heads):
+                packed[i, u, h] = rows[:, h * DH : (h + 1) * DH]
+            return 0
+
+        lax.fori_loop(0, slots, one, 0)
+        if i + 2 < pieces:
+            stage(i + 2).start()
+        mine = pl.ds(CAP * me, CAP)
+        arrived[i][mine] = packed[i, mine]
+
+    def remote(i, off):
+        to = lax.rem(me + off, n)
+        return pltpu.make_async_remote_copy(
+            src_ref=packed.at[i, pl.ds(CAP * to, CAP)],
+            dst_ref=arrived[i].at[pl.ds(CAP * me, CAP)],
+            send_sem=send_sem.at[i, off - 1],
+            recv_sem=recv_sem.at[i, off - 1],
+            device_id={"ctx": to},
+            device_id_type=MESH,
+        )
+
+    def each_peer(i, action):
+        def one(off, _):
+            action(remote(i, off))
+            return 0
+
+        lax.fori_loop(1, n, one, 0)
+
+    def unpack(i, target):
+        def one(u, _):
+            rows = pl.ds(pl.multiple_of(u * unit_rows, unit_rows), unit_rows)
+            target[:, rows, :] = arrived[i][lookup[u]]
+            return 0
+
+        lax.fori_loop(0, slots, one, 0)
+
+    def chain(g):
+        return pltpu.make_async_remote_copy(
+            src_ref=chain_out.at[g],
+            dst_ref=chain_in.at[g],
+            send_sem=chain_send.at[g],
+            recv_sem=chain_recv.at[g],
+            device_id={"ctx": lax.rem(me + 1, n)},
+            device_id_type=MESH,
+        )
+
+    def states(g):
+        each_peer(2 * g, lambda c: c.wait_recv())
+        each_peer(2 * g + 1, lambda c: c.wait_recv())
+        unpack(2 * g, k_ord)
+        unpack(2 * g + 1, v_ord)
+        for b in range(blocks):
+            rows = slice(b * BLK, (b + 1) * BLK)
+            last = doc_col[(b + 1) * BLK - 1 : (b + 1) * BLK, :]
+            recent = doc_col[rows, :] == last
+
+            def one(h, _):
+                keys = jnp.where(recent, k_ord[h, rows, :], 0.0).astype(jnp.bfloat16)
+                block_state[g, b, h] = lax.dot_general(
+                    keys, v_ord[h, rows, :], (((0,), (0,)), ((), ())),
+                    preferred_element_type=jnp.float32,
+                )
+                return 0
+
+            lax.fori_loop(0, group_heads, one, 0)
+
+        @pl.when(me == 0)
+        def _():
+            chain_in[g] = jnp.zeros_like(chain_in[g])
+
+        @pl.when(me > 0)
+        def _():
+            chain(g).wait_recv()
+
+        @pl.when(me < n - 1)
+        def _():
+            running = chain_in[g].astype(jnp.float32)
+            for b in range(blocks):
+                running = flags[0, b] * running + block_state[g, b]
+            chain_out[g] = running.astype(jnp.bfloat16)
+            chain(g).start()
+
+    def out_copy(g):
+        return pltpu.make_async_copy(
+            out_buf.at[g % 2], out.at[:, pl.ds(g * width, width)], out_sem.at[g % 2]
+        )
+
+    def attend(g):
+        each_peer(2 * GROUPS + g, lambda c: c.wait_recv())
+        unpack(2 * GROUPS + g, q_ord)
+        unpack(2 * g, k_ord)
+        unpack(2 * g + 1, v_ord)
+        if g >= 2:
+            out_copy(g - 2).wait()
+        for b in range(blocks):
+            for t in range(BLK // TILE):
+                first = b * BLK
+                rows = slice(first + t * TILE, first + (t + 1) * TILE)
+                keys = slice(first, first + (t + 1) * TILE)
+                span = (t + 1) * TILE
+                here = doc_col[rows, :]
+                causal = lax.broadcasted_iota(jnp.int32, (TILE, span), 1) <= (
+                    lax.broadcasted_iota(jnp.int32, (TILE, span), 0) + t * TILE
+                )
+                allowed = causal & (here[:, :1] == doc_row[:1, keys])
+                seen = here == doc_col[first : first + 1, :]
+
+                def one(h, _):
+                    running = chain_in[g, h].astype(jnp.float32)
+                    for p in range(b):
+                        running = flags[0, p] * running + block_state[g, p, h]
+                    entering = (flags[1, b] * running).astype(jnp.bfloat16)
+                    query = q_ord[h, rows, :]
+                    scores = lax.dot_general(
+                        query, k_ord[h, keys, :], (((1,), (1,)), ((), ())),
+                        preferred_element_type=jnp.float32,
+                    )
+                    weights = jnp.where(allowed, scores, 0.0).astype(jnp.bfloat16)
+                    within = jnp.dot(
+                        weights, v_ord[h, keys, :], preferred_element_type=jnp.float32
+                    )
+                    carried = jnp.dot(query, entering, preferred_element_type=jnp.float32)
+                    total = within + jnp.where(seen, carried, 0.0)
+                    squares[rows, :] += total * total
+                    columns = pl.ds(pl.multiple_of(h * DH, DH), DH)
+                    out_buf[g % 2, rows, columns] = total.astype(jnp.bfloat16)
+                    return 0
+
+                lax.fori_loop(0, group_heads, one, 0)
+        out_copy(g).start()
+
+    def tp_copy(off):
+        return pltpu.make_async_remote_copy(
+            src_ref=own_sum,
+            dst_ref=tp_in.at[off - 1],
+            send_sem=tp_send.at[off - 1],
+            recv_sem=tp_recv.at[off - 1],
+            device_id={"tp": lax.rem(my_tp + off, tp)},
+            device_id_type=MESH,
+        )
+
+    barrier = pltpu.get_barrier_semaphore()
+    stage(0).start()
+    stage(1).start()
+
+    def greet_ctx(off, _):
+        pl.semaphore_signal(
+            barrier, inc=1, device_id={"ctx": lax.rem(me + off, n)}, device_id_type=MESH
+        )
+        return 0
+
+    def greet_tp(off, _):
+        pl.semaphore_signal(
+            barrier, inc=1, device_id={"tp": lax.rem(my_tp + off, tp)}, device_id_type=MESH
+        )
+        return 0
+
+    lax.fori_loop(1, n, greet_ctx, 0)
+    lax.fori_loop(1, tp, greet_tp, 0)
+    prepare(0)
+    pl.semaphore_wait(barrier, n - 1 + tp - 1)
+    squares[...] = jnp.zeros_like(squares)
+
+    for i in range(pieces):
+        if i > 0:
+            prepare(i)
+        if i >= WINDOW:
+            each_peer(i - WINDOW, lambda c: c.wait_send())
+        each_peer(i, lambda c: c.start())
+        done = i - WINDOW
+        if 0 <= done < 2 * GROUPS and done % 2 == 1:
+            states(done // 2)
+        elif done >= 2 * GROUPS:
+            attend(done - 2 * GROUPS)
+    for i in range(pieces - WINDOW, pieces):
+        attend(i - 2 * GROUPS)
+    own_sum[...] = lax.dot_general(
+        jnp.ones((8, DH), jnp.float32), squares[...], (((1,), (1,)), ((), ())),
+        preferred_element_type=jnp.float32, precision=lax.Precision.HIGHEST,
+    )
+    for off in range(1, tp):
+        tp_copy(off).start()
+    for i in range(pieces - WINDOW, pieces):
+        each_peer(i, lambda c: c.wait_send())
+
+    @pl.when(me < n - 1)
+    def _():
+        for g in range(GROUPS):
+            chain(g).wait_send()
+
+    for g in range(max(GROUPS - 2, 0), GROUPS):
+        out_copy(g).wait()
+    total = own_sum[...]
+    for off in range(1, tp):
+        tp_copy(off).wait_recv()
+        total = total + tp_in[off - 1]
+    for off in range(1, tp):
+        tp_copy(off).wait_send()
+    sums[...] = total
+
+
+def fused(queries, keys, values, gain, starts, source_unit):
+    n = lax.axis_size("ctx")
+    tp = lax.axis_size("tp")
+    my_index = lax.axis_index("ctx")
+    tokens, columns = queries.shape
+    slots = CAP * n
+    unit_rows = tokens // slots
+    heads = columns // DH
+    group_heads = heads // GROUPS
+    blocks = tokens // BLK
+    owners = source_unit.reshape(n, slots)
+    source_shard = owners // slots
+    source_slot = owners % slots
+    earlier = jnp.arange(slots)[None, :] < jnp.arange(slots)[:, None]
+    same_source = source_shard[:, :, None] == source_shard[:, None, :]
+    rank = jnp.sum(jnp.where(same_source & earlier[None], 1, 0), axis=2).astype(jnp.int32)
+    matches = (source_shard == my_index)[:, None, :] & (
+        rank[:, None, :] == jnp.arange(CAP, dtype=jnp.int32)[None, :, None]
+    )
+    chosen = jnp.sum(jnp.where(matches, source_slot[:, None, :], 0), axis=2).reshape(-1)
+    lookup = lax.dynamic_index_in_dim(source_shard * CAP + rank, my_index, 0, keepdims=False)
+    doc = jnp.cumsum(starts).astype(jnp.int32)
+    block_starts = starts.reshape(blocks, BLK)
+    flags = jnp.stack(
+        [jnp.where(jnp.any(block_starts > 0, axis=1), 0.0, 1.0),
+         jnp.where(block_starts[:, 0] > 0, 0.0, 1.0)]
+    ).astype(jnp.float32)
+    doc_col = jnp.broadcast_to(doc[:, None], (tokens, DH))
+    doc_row = jnp.broadcast_to(doc[None, :], (8, tokens))
+    pieces = 3 * GROUPS
+    piece = (slots, group_heads, unit_rows, DH)
+    bf16, f32 = jnp.bfloat16, jnp.float32
+    hbm = pl.BlockSpec(memory_space=pl.ANY)
+    smem = pl.BlockSpec(memory_space=pltpu.SMEM)
+    vmem = pl.BlockSpec(memory_space=pltpu.VMEM)
+    ordered = pltpu.VMEM((group_heads, tokens, DH), bf16)
+    dma = pltpu.SemaphoreType.DMA
+    attended, sums = pl.pallas_call(
+        functools.partial(exchange_kernel, n, tp),
+        out_shape=(
+            jax.ShapeDtypeStruct((tokens, columns), bf16),
+            jax.ShapeDtypeStruct((8, tokens), f32),
+        ),
+        in_specs=[hbm, hbm, hbm, smem, smem, smem, vmem, vmem],
+        out_specs=(hbm, vmem),
+        scratch_shapes=[
+            [pltpu.VMEM((slots, unit_rows, group_heads * DH), bf16) for _ in range(2)],
+            pltpu.VMEM((pieces,) + piece, bf16),
+            [pltpu.VMEM(piece, bf16) for _ in range(pieces)],
+            ordered, ordered, ordered,
+            pltpu.VMEM((GROUPS, group_heads, DH, DH), bf16),
+            pltpu.VMEM((GROUPS, group_heads, DH, DH), bf16),
+            pltpu.VMEM((GROUPS, blocks, group_heads, DH, DH), f32),
+            pltpu.VMEM((2, tokens, group_heads * DH), bf16),
+            pltpu.VMEM((tokens, DH), f32),
+            pltpu.VMEM((8, tokens), f32),
+            pltpu.VMEM((max(tp - 1, 1), 8, tokens), f32),
+            dma((2,)),
+            dma((pieces, n - 1)),
+            dma((pieces, n - 1)),
+            dma((GROUPS,)),
+            dma((GROUPS,)),
+            dma((2,)),
+            dma((max(tp - 1, 1),)),
+            dma((max(tp - 1, 1),)),
+        ],
+        compiler_params=pltpu.CompilerParams(
+            collective_id=0, has_side_effects=True, vmem_limit_bytes=62 * 1024 * 1024
+        ),
+    )(
+        queries.reshape(slots, unit_rows, columns),
+        keys.reshape(slots, unit_rows, columns),
+        values.reshape(slots, unit_rows, columns),
+        chosen, lookup, flags, doc_col, doc_row,
+    )
+    mean_square = sums[0] / (columns * tp)
+    scale = lax.rsqrt(mean_square + 1e-06)[:, None]
+    return (attended.astype(f32) * scale * gain).astype(bf16)
 
 
 def local(queries, keys, values, gain, starts, source_unit):
@@ -104,4 +429,10 @@
 def solution(mesh):
     in_specs = (P("ctx", "tp"), P("ctx", "tp"), P("ctx", "tp"), P("tp"), P("ctx"), P())
     out_specs = P("ctx", "tp")
-    return jax.shard_map(local, mesh=mesh, in_specs=in_specs, out_specs=out_specs, check_vma=False)
+
+    def body(queries, keys, values, gain, starts, source_unit):
+        unit_rows = queries.shape[0] // (CAP * mesh.shape["ctx"])
+        whole = unit_rows % 16 == 0 and queries.shape[1] % (GROUPS * DH) == 0
+        return (fused if whole else local)(queries, keys, values, gain, starts, source_unit)
+
+    return jax.shard_map(body, mesh=mesh, in_specs=in_specs, out_specs=out_specs, check_vma=False)

time: 668 us -> 504 us (0.75)
  Pallas kernels: 0 us -> 489 us
  blocking collectives: 311 us -> 0 us
  waiting for transfers between devices: 118 us -> 0 us
  local copies, waits for them, and re-layouts: 100 us -> 4.6 us
  other arithmetic: 58.3 us -> 10.2 us
  matrix products: 46.9 us -> 0 us
  between operations: 14.2 us -> 0.05 us
  starting transfers between devices: 13.6 us -> 0 us
    pallas_call x0 -> x1, Pallas kernels: none -> 489 us  [fused(): pl.pallas_call(functools.partial(exchange_kernel, n, tp), out_shape=(jax....]
    unnamed x1 -> x0, blocking collectives: 161 us -> none
    all_to_all x1 -> x0, blocking collectives: 141 us -> none  [local(): lax.all_to_all(packed(keys), 'ctx', split_axis=0, concat_axis=0, tiled=True)]
    all_to_all x2 -> x0, waiting for transfers between devices: 118 us -> none  [the longest x1 118 us: local(): lax.all_to_all(packed(values), 'ctx', split_axis=0, concat_axis=0, tiled=...]
    dot_general x4 -> x0, matrix products: 46.9 us -> none  [the longest x1 30.5 us: local(): jnp.einsum('bhts,bshe->bthe', weights, v_bal, preferred_element_type=jnp....]
    gather x6 -> x0, local copies, waits for them, and re-layouts: 38.4 us -> none  [the longest x3 19.2 us: packed(): pieces = array.reshape(slot_count, unit_rows, column_count)[chosen]]
    unnamed x19 -> x2, local copies, waits for them, and re-layouts: 23.9 us -> 0.01 us
    select_n x5 -> x3, other arithmetic: 23.6 us -> 0.13 us  [the longest x1 0.12 us: fused(): jnp.where(block_starts[:, 0] > 0, 0.0, 1.0)]
  transfers between devices with their start and end apart: 3 -> 0, of which waited for: 1 -> 0; matrix products, arithmetic and copies ran while one was open for 16% -> 0% of each run, Pallas kernels for 0% -> 0%
where the time goes in v1:
time: 504 us
  Pallas kernels  489 us (97%)
  other arithmetic  10.2 us (2%)
    pallas_call x1, Pallas kernels, fused(): pl.pallas_call(functools.partial(exchange_kernel, n, tp), out_shape=(jax....  489 us

profile of v1, /device:TPU:13, one launch (start us, length us, event | category | flops | bytes accessed | tf_op | source)
XLA Modules:
  0.0 503.9 jit_solution(3953196739804525730)
XLA Ops:
  0.0 0.7 reshape.198
  0.8 0.3 select_reduce_fusion
  1.1 0.2 select_reduce_fusion.1
  1.2 0.5 dynamic-slice_bitcast_fusion.lookup
  1.7 0.1 copy.7
  1.8 0.6 reshape.199.chosen
  2.4 0.7 reshape.200
  3.1 0.1 fusion.3
  3.2 0.1 compare_reduce_fusion
  3.4 0.6 pad_maximum_fusion.flags
  4.0 1.0 reduce-window.9
  4.9 0.1 slice.18
  5.0 0.1 slice_reduce_fusion
  5.2 0.1 add_bitcast_fusion
  5.2 0.6 broadcast_in_dim.66.doc_row
  5.9 1.1 broadcast_in_dim.65.doc_col
  7.0 0.0 copy-start
  7.0 489.1 %shard_map.64 = (bf16[1536,2048]{1,0:T(8,128)(2,1)}, f32[8,1536]{1,0:T(8,128)}) custom-call(bf16[16,96,2048]{2,1,0:T(8,128)(2,1)} %bitcast.11, bf16[16,96,2048]{2,1,0:T(8,128)(2,1)} %bitcast.12, bf16[16,96,2048]{2,1,0:T(8,128)(2,1)} %bitcast.13, s32[16]{0:T(128)} %reshape.199.chosen, s32[16]{0:T(128)} %dynamic-slice_bitcast_fusion.lookup, ...), custom_call_target="tpu_custom_call" | custom-call | tf_op jit(solution)/shard_map/pallas_call | solution.py:293
  496.1 0.8 rsqrt_reduce_fusion
  497.0 0.0 copy-done
  497.0 7.0 %multiply_convert_fusion = bf16[1536,2048]{1,0:T(8,128)(2,1)} fusion(bf16[1536,2048]{1,0:T(8,128)(2,1)} %get-tuple-element.7, f32[2048]{0:T(1024)S(1)} %copy-done, f32[1536]{0:T(1024)S(1)} %rsqrt_reduce_fusion), kind=kLoop, calls=%fused_computation | loop fusion | flops 12582912 | bytes 12597248 | tf_op jit(solution)/shard_map/convert_element_type | solution.py:333
  (6 shorter events, 0.1 us)
Async XLA Ops:
  7.0 490.0 %copy-start = (f32[2048]{0:T(1024)S(1)}, f32[2048]{0:T(1024)}, u32[]{:S(2)}) copy-start(f32[2048]{0:T(1024)} %param.9) | copy-start | bytes 24580

commit v2 on v1

--- a/solution.py
+++ b/solution.py
@@ -10,8 +10,9 @@
 CAP = 2
 BLK = 768
 TILE = 256
-GROUPS = 4
-WINDOW = 2
+GROUPS = 8
+WINDOW = 4
+STAGGER = 5
 MESH = pl.DeviceIdType.MESH
 
 
@@ -62,13 +63,19 @@
         mine = pl.ds(CAP * me, CAP)
         arrived[i][mine] = packed[i, mine]
 
+    half = n // 2
+    side, place = me // half, lax.rem(me, half)
+
     def remote(i, off):
-        to = lax.rem(me + off, n)
+        turn = lax.rem(off - 1 + lax.rem(my_tp, 2), n - 1)
+        other = 1 - lax.rem(turn, 2)
+        step = (turn + 1) // 2
+        to = lax.rem(side + other, 2) * half + lax.rem(place + step, half)
         return pltpu.make_async_remote_copy(
             src_ref=packed.at[i, pl.ds(CAP * to, CAP)],
             dst_ref=arrived[i].at[pl.ds(CAP * me, CAP)],
-            send_sem=send_sem.at[i, off - 1],
-            recv_sem=recv_sem.at[i, off - 1],
+            send_sem=send_sem.at[i, turn],
+            recv_sem=recv_sem.at[i, turn],
             device_id={"ctx": to},
             device_id_type=MESH,
         )
@@ -118,10 +125,7 @@
 
             lax.fori_loop(0, group_heads, one, 0)
 
-        @pl.when(me == 0)
-        def _():
-            chain_in[g] = jnp.zeros_like(chain_in[g])
-
+    def pass_on(g):
         @pl.when(me > 0)
         def _():
             chain(g).wait_recv()
@@ -193,6 +197,19 @@
             device_id_type=MESH,
         )
 
+    def follow(done):
+        if 0 <= done < 2 * GROUPS and done % 2 == 1:
+            states(done // 2)
+        if 1 <= done < 2 * GROUPS + STAGGER:
+            late = done - 1 - me * STAGGER // n
+
+            @pl.when((late >= 0) & (lax.rem(late, 2) == 0) & (late < 2 * GROUPS))
+            def _():
+                pass_on(late // 2)
+
+        if done >= 2 * GROUPS:
+            attend(done - 2 * GROUPS)
+
     barrier = pltpu.get_barrier_semaphore()
     stage(0).start()
     stage(1).start()
@@ -214,6 +231,11 @@
     prepare(0)
     pl.semaphore_wait(barrier, n - 1 + tp - 1)
     squares[...] = jnp.zeros_like(squares)
+
+    @pl.when(me == 0)
+    def _():
+        chain_in[...] = jnp.zeros_like(chain_in)
+
 
     for i in range(pieces):
         if i > 0:
@@ -221,13 +243,9 @@
         if i >= WINDOW:
             each_peer(i - WINDOW, lambda c: c.wait_send())
         each_peer(i, lambda c: c.start())
-        done = i - WINDOW
-        if 0 <= done < 2 * GROUPS and done % 2 == 1:
-            states(done // 2)
-        elif done >= 2 * GROUPS:
-            attend(done - 2 * GROUPS)
+        follow(i - WINDOW)
     for i in range(pieces - WINDOW, pieces):
-        attend(i - 2 * GROUPS)
+        follow(i)
     own_sum[...] = lax.dot_general(
         jnp.ones((8, DH), jnp.float32), squares[...], (((1,), (1,)), ((), ())),
         preferred_element_type=jnp.float32, precision=lax.Precision.HIGHEST,

time: 504 us -> 478 us (0.948)
  Pallas kernels: 489 us -> 463 us
    pallas_call x1, Pallas kernels: 489 us -> 463 us  [fused(): pl.pallas_call(functools.partial(exchange_kernel, n, tp), out_shape=(jax....]
where the time goes in v2:
time: 478 us
  Pallas kernels  463 us (97%)
  other arithmetic  10.2 us (2%)
    pallas_call x1, Pallas kernels, fused(): pl.pallas_call(functools.partial(exchange_kernel, n, tp), out_shape=(jax....  463 us

profile of v2, /device:TPU:13, one launch (start us, length us, event | category | flops | bytes accessed | tf_op | source)
XLA Modules:
  0.0 478.0 jit_solution(4773927140796032071)
XLA Ops:
  0.0 0.7 reshape.198
  0.8 0.3 select_reduce_fusion
  1.1 0.2 select_reduce_fusion.1
  1.2 0.5 dynamic-slice_bitcast_fusion.lookup
  1.7 0.1 copy.7
  1.8 0.6 reshape.199.chosen
  2.4 0.7 reshape.200
  3.1 0.1 fusion.3
  3.2 0.1 compare_reduce_fusion
  3.4 0.6 pad_maximum_fusion.flags
  4.0 1.0 reduce-window.9
  4.9 0.1 slice.18
  5.0 0.1 slice_reduce_fusion
  5.2 0.1 add_bitcast_fusion
  5.2 0.6 broadcast_in_dim.66.doc_row
  5.9 1.1 broadcast_in_dim.65.doc_col
  7.0 0.0 copy-start
  7.0 463.1 %shard_map.64 = (bf16[1536,2048]{1,0:T(8,128)(2,1)}, f32[8,1536]{1,0:T(8,128)}) custom-call(bf16[16,96,2048]{2,1,0:T(8,128)(2,1)} %bitcast.11, bf16[16,96,2048]{2,1,0:T(8,128)(2,1)} %bitcast.12, bf16[16,96,2048]{2,1,0:T(8,128)(2,1)} %bitcast.13, s32[16]{0:T(128)} %reshape.199.chosen, s32[16]{0:T(128)} %dynamic-slice_bitcast_fusion.lookup, ...), custom_call_target="tpu_custom_call" | custom-call | tf_op jit(solution)/shard_map/pallas_call | solution.py:311
  470.2 0.8 rsqrt_reduce_fusion
  471.0 0.0 copy-done
  471.0 7.0 %multiply_convert_fusion = bf16[1536,2048]{1,0:T(8,128)(2,1)} fusion(bf16[1536,2048]{1,0:T(8,128)(2,1)} %get-tuple-element.7, f32[2048]{0:T(1024)S(1)} %copy-done, f32[1536]{0:T(1024)S(1)} %rsqrt_reduce_fusion), kind=kLoop, calls=%fused_computation | loop fusion | flops 12582912 | bytes 12597248 | tf_op jit(solution)/shard_map/convert_element_type | solution.py:351
  (6 shorter events, 0.1 us)
Async XLA Ops:
  7.0 464.0 %copy-start = (f32[2048]{0:T(1024)S(1)}, f32[2048]{0:T(1024)}, u32[]{:S(2)}) copy-start(f32[2048]{0:T(1024)} %param.9) | copy-start | bytes 24580

commit v3 on v2

--- a/solution.py
+++ b/solution.py
@@ -11,8 +11,8 @@
 BLK = 768
 TILE = 256
 GROUPS = 8
-WINDOW = 4
-STAGGER = 5
+WINDOW = 6
+STAGGER = 8
 MESH = pl.DeviceIdType.MESH
 
 

time: 478 us -> 480 us (level)
  no operation moved by 1% of the time
where the time goes in v3:
time: 480 us; the launch traced here: 479 us
  Pallas kernels  464 us (97%)
  other arithmetic  10.2 us (2%)
    pallas_call x1, Pallas kernels, fused(): pl.pallas_call(functools.partial(exchange_kernel, n, tp), out_shape=(jax....  464 us

profile of v3, /device:TPU:13, one launch (start us, length us, event | category | flops | bytes accessed | tf_op | source)
XLA Modules:
  0.0 479.3 jit_solution(15011562589399228828)
XLA Ops:
  0.0 0.7 reshape.198
  0.8 0.3 select_reduce_fusion
  1.1 0.2 select_reduce_fusion.1
  1.2 0.5 dynamic-slice_bitcast_fusion.lookup
  1.7 0.1 copy.7
  1.8 0.6 reshape.199.chosen
  2.4 0.7 reshape.200
  3.1 0.1 fusion.3
  3.2 0.1 compare_reduce_fusion
  3.4 0.6 pad_maximum_fusion.flags
  4.0 1.0 reduce-window.9
  4.9 0.1 slice.18
  5.0 0.1 slice_reduce_fusion
  5.2 0.1 add_bitcast_fusion
  5.2 0.6 broadcast_in_dim.66.doc_row
  5.9 1.1 broadcast_in_dim.65.doc_col
  7.0 0.0 copy-start
  7.0 464.5 %shard_map.64 = (bf16[1536,2048]{1,0:T(8,128)(2,1)}, f32[8,1536]{1,0:T(8,128)}) custom-call(bf16[16,96,2048]{2,1,0:T(8,128)(2,1)} %bitcast.11, bf16[16,96,2048]{2,1,0:T(8,128)(2,1)} %bitcast.12, bf16[16,96,2048]{2,1,0:T(8,128)(2,1)} %bitcast.13, s32[16]{0:T(128)} %reshape.199.chosen, s32[16]{0:T(128)} %dynamic-slice_bitcast_fusion.lookup, ...), custom_call_target="tpu_custom_call" | custom-call | tf_op jit(solution)/shard_map/pallas_call | solution.py:311
  471.5 0.8 rsqrt_reduce_fusion
  472.3 0.0 copy-done
  472.3 7.0 %multiply_convert_fusion = bf16[1536,2048]{1,0:T(8,128)(2,1)} fusion(bf16[1536,2048]{1,0:T(8,128)(2,1)} %get-tuple-element.7, f32[2048]{0:T(1024)S(1)} %copy-done, f32[1536]{0:T(1024)S(1)} %rsqrt_reduce_fusion), kind=kLoop, calls=%fused_computation | loop fusion | flops 12582912 | bytes 12597248 | tf_op jit(solution)/shard_map/convert_element_type | solution.py:351
  (6 shorter events, 0.1 us)
Async XLA Ops:
  7.0 465.3 %copy-start = (f32[2048]{0:T(1024)S(1)}, f32[2048]{0:T(1024)}, u32[]{:S(2)}) copy-start(f32[2048]{0:T(1024)} %param.9) | copy-start | bytes 24580

commit v4 on v3

--- a/solution.py
+++ b/solution.py
@@ -11,7 +11,7 @@
 BLK = 768
 TILE = 256
 GROUPS = 8
-WINDOW = 6
+WINDOW = 4
 STAGGER = 8
 MESH = pl.DeviceIdType.MESH
 

time: 480 us -> 467 us (0.973)
  Pallas kernels: 464 us -> 448 us
    pallas_call x1, Pallas kernels: 464 us -> 448 us  [fused(): pl.pallas_call(functools.partial(exchange_kernel, n, tp), out_shape=(jax....]
where the time goes in v4:
time: 467 us; the launch traced here: 463 us
  Pallas kernels  448 us (96%)
  other arithmetic  10.2 us (2%)
    pallas_call x1, Pallas kernels, fused(): pl.pallas_call(functools.partial(exchange_kernel, n, tp), out_shape=(jax....  448 us

profile of v4, /device:TPU:13, one launch (start us, length us, event | category | flops | bytes accessed | tf_op | source)
XLA Modules:
  0.0 462.9 jit_solution(8461872247279544190)
XLA Ops:
  0.0 0.7 reshape.198
  0.8 0.3 select_reduce_fusion
  1.1 0.2 select_reduce_fusion.1
  1.2 0.5 dynamic-slice_bitcast_fusion.lookup
  1.7 0.1 copy.7
  1.8 0.6 reshape.199.chosen
  2.4 0.7 reshape.200
  3.1 0.1 fusion.3
  3.2 0.1 compare_reduce_fusion
  3.4 0.6 pad_maximum_fusion.flags
  4.0 1.0 reduce-window.9
  4.9 0.1 slice.18
  5.0 0.1 slice_reduce_fusion
  5.2 0.1 add_bitcast_fusion
  5.2 0.6 broadcast_in_dim.66.doc_row
  5.9 1.1 broadcast_in_dim.65.doc_col
  7.0 0.0 copy-start
  7.0 448.0 %shard_map.64 = (bf16[1536,2048]{1,0:T(8,128)(2,1)}, f32[8,1536]{1,0:T(8,128)}) custom-call(bf16[16,96,2048]{2,1,0:T(8,128)(2,1)} %bitcast.11, bf16[16,96,2048]{2,1,0:T(8,128)(2,1)} %bitcast.12, bf16[16,96,2048]{2,1,0:T(8,128)(2,1)} %bitcast.13, s32[16]{0:T(128)} %reshape.199.chosen, s32[16]{0:T(128)} %dynamic-slice_bitcast_fusion.lookup, ...), custom_call_target="tpu_custom_call" | custom-call | tf_op jit(solution)/shard_map/pallas_call | solution.py:311
  455.0 0.8 rsqrt_reduce_fusion
  455.9 0.0 copy-done
  455.9 7.0 %multiply_convert_fusion = bf16[1536,2048]{1,0:T(8,128)(2,1)} fusion(bf16[1536,2048]{1,0:T(8,128)(2,1)} %get-tuple-element.7, f32[2048]{0:T(1024)S(1)} %copy-done, f32[1536]{0:T(1024)S(1)} %rsqrt_reduce_fusion), kind=kLoop, calls=%fused_computation | loop fusion | flops 12582912 | bytes 12597248 | tf_op jit(solution)/shard_map/convert_element_type | solution.py:351
  (6 shorter events, 0.1 us)
Async XLA Ops:
  7.0 448.9 %copy-start = (f32[2048]{0:T(1024)S(1)}, f32[2048]{0:T(1024)}, u32[]{:S(2)}) copy-start(f32[2048]{0:T(1024)} %param.9) | copy-start | bytes 24580
